TPU v7x, 32 devices: a whole 2x2x4 slice. The times are simulated.
32 devices in a mesh: bond: 4 (over x, core), op: 8 (over z, y).
Axes of the slice: x: 2, y: 2, z: 4, core: 2. Of those that a mesh axis runs over, the one named last changes fastest.
Arguments:
- wave_slab: bfloat16 [8192, 8192], P('op', 'bond'), may hold values from -6 to 6
- left_blocks: bfloat16 [16, 16, 2, 128, 128], P('op'), may hold values from -0.375 to 0.375
- right_blocks: bfloat16 [16, 64, 2, 128, 128], P('op'), may hold values from -0.09375 to 0.09375
- sector_size: int32 [64], replicated, may hold values from 1 to 128
- left_pairs: int32 [16, 16, 2], P('op'), may hold values from 0 to 63
- right_pairs: int32 [16, 64, 2], P('op'), may hold values from 0 to 63
Outputs:
- applied: float32 [2048, 8192], P('bond', 'op')
All inputs are finite; a program needn't handle non-finite values.
Results may differ from a plain program's by a relative error of at most 0.0029.
Values may be sent and summed in bfloat16 or wider, within the bound.
A program may use at most 128 MiB of HBM per device.

v0:
```python
import jax
import jax.numpy as jnp
from jax import lax
from jax.sharding import PartitionSpec as P

TILE = 128


def live_mask(sector_size):
    states = jnp.arange(TILE, dtype=jnp.int32)
    return (states[None, :] < sector_size[:, None]).astype(jnp.float32).reshape(-1)


def on_device(wave_slab, left_blocks, right_blocks, sector_size, left_pairs, right_pairs):
    live = live_mask(sector_size)
    local_rows = wave_slab.shape[0]
    strip = wave_slab.shape[1]
    row_live = lax.dynamic_slice_in_dim(live, lax.axis_index("op") * local_rows, local_rows)
    col_live = lax.dynamic_slice_in_dim(live, lax.axis_index("bond") * strip, strip)
    masked = (wave_slab.astype(jnp.float32) * row_live[:, None] * col_live[None, :]).astype(
        jnp.bfloat16
    )
    whole = lax.all_gather(masked, "op", axis=0, tiled=True)
    full_width = whole.shape[0]
    sector_count = full_width // TILE
    sectors = whole.reshape(sector_count, TILE, strip)
    term_count = left_blocks.shape[0]
    middles = []
    for term_idx in range(term_count):
        picked = sectors[left_pairs[term_idx]]
        middle = jnp.einsum(
            "ipxy,ipys->ixs", left_blocks[term_idx], picked, preferred_element_type=jnp.float32
        )
        middles.append(middle.astype(jnp.bfloat16).reshape(-1, strip))
    stacked = jnp.stack(middles, 0)
    bond_count = lax.axis_size("bond")
    slab_rows = stacked.shape[1]
    share_rows = slab_rows // bond_count
    blocked = stacked.reshape(term_count, bond_count, share_rows, strip)
    arrived = lax.all_to_all(blocked, "bond", split_axis=1, concat_axis=3, tiled=True)
    row_count = arrived.shape[2]
    total = jnp.zeros((row_count, sector_count, TILE), jnp.float32)
    for term_idx in range(term_count):
        split_cols = arrived[term_idx, 0].reshape(row_count, sector_count, TILE)
        chosen = split_cols[:, right_pairs[term_idx]]
        total = total + jnp.einsum(
            "rjpy,jpyz->rjz", chosen, right_blocks[term_idx], preferred_element_type=jnp.float32
        )
    partial_value = total.reshape(row_count, full_width)
    summed = lax.psum_scatter(partial_value, "op", scatter_dimension=1, tiled=True)
    out_cols = summed.shape[1]
    out_row_live = lax.dynamic_slice_in_dim(live, lax.axis_index("bond") * share_rows, share_rows)
    out_col_live = lax.dynamic_slice_in_dim(live, lax.axis_index("op") * out_cols, out_cols)
    return summed * out_row_live[:, None] * out_col_live[None, :]


def solution(mesh):
    placed = (
        P("op", "bond"),
        P("op", None, None, None, None),
        P("op", None, None, None, None),
        P(),
        P("op", None, None),
        P("op", None, None),
    )
    return jax.shard_map(
        on_device, mesh=mesh, in_specs=placed, out_specs=P("bond", "op"), check_vma=False
    )
```

profile of v0, /device:TPU:13, one launch (start us, length us, event | category | flops | bytes accessed | tf_op | source)
XLA Modules:
  0.0 1327.5 jit_solution(17087436077110806129)
XLA Ops:
  6.5 0.0 all-gather.2.cloned.1.call-start
  6.5 0.7 convert_bitcast_fusion
  7.3 0.0 copy-start.1
  7.3 0.0 copy-start.2
  7.3 0.6 copy-done.2
  7.9 5.3 multiply_convert_fusion
  13.2 0.0 all-gather.2.cloned.1.call-update
  13.2 0.7 compare_select_fusion.3
  13.9 0.1 copy.25
  14.0 0.1 reshape.143
  14.1 0.1 copy.26
  14.2 0.1 reshape.151
  14.3 637.0 %all-gather.2.cloned.1.call-done = bf16[8192,2048]{1,0:T(8,128)(2,1)} async-done(((bf16[1024,2048]{1,0:T(8,128)(2,1)}), bf16[8192,2048]{1,0:T(8,128)(2,1)}) %all-gather.2.cloned.1.call-update) | async-done | bytes 33554448 | tf_op jit(solution)/shard_map/all_gather | solution.py:23
  651.3 0.0 copy-done.1
  651.3 0.0 copy-start
  651.3 12.2 gather_fusion
  663.6 0.0 copy-done
  663.6 11.3 bitcast_convert_fusion.1
  674.9 11.4 copy.27
  686.4 11.7 gather_fusion.1
  698.1 11.4 bitcast_convert_fusion
  709.4 11.4 copy.28
  720.9 13.7 %pad_maximum_fusion = bf16[2,4,512,2048]{2,3,0,1:T(8,128)(2,1)} fusion(bf16[1,4,512,2048]{2,3,0,1:T(8,128)(2,1)} %copy.28, bf16[1,4,512,2048]{2,3,0,1:T(8,128)(2,1)} %copy.27), kind=kLoop, calls=%fused_computation.4 | loop fusion | flops 8388608 | bytes 33554432 | tf_op jit(solution)/shard_map/stack | solution.py:35
  734.6 0.0 copy-start.4
  734.6 7.7 all-to-all-start
  742.3 0.0 reduce-scatter.2.cloned.1.call-start
  742.3 0.0 copy-done.4
  742.4 0.1 copy.30
  742.5 0.1 reshape.159
  742.6 0.1 copy.33
  742.7 0.1 reshape.167
  742.9 181.7 %all-to-all-done = bf16[2,4,512,2048]{2,3,0,1:T(8,128)(2,1)} async-done(((bf16[2,4,512,2048]{2,3,0,1:T(8,128)(2,1)}), bf16[2,4,512,2048]{2,3,0,1:T(8,128)(2,1)}, u32[]{:S(2)}, u32[]{:S(2)}) %all-to-all-start) | async-done | bytes 16777248 | tf_op jit(solution)/shard_map/all_to_all | solution.py:40
  924.6 8.0 copy.44
  932.6 6.1 fusion.9
  938.6 11.9 copy.31
  950.6 11.9 copy.34
  962.5 11.7 gather_fusion.2
  974.2 13.7 %fusion.1 = f32[64,512,128,1]{1,2,3,0:T(8,128)} fusion(bf16[512,64,2,128]{3,0,2,1:T(8,128)(2,1)} %bitcast.73, bf16[2,64,2,128,128]{4,3,2,1,0:T(8,128)(2,1)} %param.8), kind=kOutput, calls=%fused_computation.11 | convolution fusion | flops 2147483648 | bytes 37748736 | tf_op jit(solution)/shard_map/rjpy,jpyz->rjz/dot_general | solution.py:46
  988.0 11.7 gather_fusion.3
  999.6 18.4 %bitcast_add_fusion = f32[64,512,128]{1,2,0:T(8,128)} fusion(f32[64,512,128,1]{1,2,3,0:T(8,128)} %fusion.1, bf16[512,64,2,128]{3,0,2,1:T(8,128)(2,1)} %bitcast.74, bf16[2,64,2,128,128]{4,3,2,1,0:T(8,128)(2,1)} %param.8), kind=kOutput, calls=%fused_computation.5 | convolution fusion | flops 2151677952 | bytes 54525952 | tf_op jit(solution)/shard_map/rjpy,jpyz->rjz/dot_general | solution.py:46
  1018.0 17.4 %copy.36 = f32[512,8192]{1,0:T(8,128)} copy(f32[512,8192]{0,1:T(8,128)} %bitcast.75) | data formatting | bytes 33554432 | tf_op jit(solution)/shard_map/reshape | solution.py:49
  1035.5 0.0 copy-start.3
  1035.5 0.0 reduce-scatter.2.cloned.1.call-update
  1035.5 0.8 dynamic_slice.12
  1036.3 281.3 %reduce-scatter.2.cloned.1.call-done = f32[512,1024]{1,0:T(8,128)} async-done(((f32[512,8192]{1,0:T(8,128)}), f32[512,1024]{1,0:T(8,128)}) %reduce-scatter.2.cloned.1.call-update) | async-done | bytes 2097168 | tf_op jit(solution)/shard_map/reduce_scatter | solution.py:50
  1317.5 0.0 copy-done.3
  1317.5 3.1 multiply_multiply_fusion
  (7 shorter events, 0.0 us)
Async XLA Ops:
  6.5 644.8 %all-gather.2.cloned.1.call-start = ((), (), s32[]{:S(2)}) async-start(), calls=%async_computation.2 | async-start | bytes 37748736 | tf_op jit(solution)/shard_map/all_gather | solution.py:23
  7.3 644.1 %copy-start.1 = (f32[8192]{0:T(1024)}, f32[8192]{0:T(1024)S(1)}, u32[]{:S(2)}) copy-start(f32[8192]{0:T(1024)S(1)} %convert_bitcast_fusion) | copy-start | bytes 98308
  7.3 0.6 copy-start.2
  651.3 12.3 copy-start
  734.6 7.7 copy-start.4
  734.6 190.0 %all-to-all-start = ((bf16[2,4,512,2048]{2,3,0,1:T(8,128)(2,1)}), bf16[2,4,512,2048]{2,3,0,1:T(8,128)(2,1)}, u32[]{:S(2)}, u32[]{:S(2)}) async-start(bf16[2,4,512,2048]{2,3,0,1:T(8,128)(2,1)} %pad_maximum_fusion), calls=%async_computation | async-start | bytes 33554432 | tf_op jit(solution)/shard_map/all_to_all | solution.py:40
  742.3 575.2 %reduce-scatter.2.cloned.1.call-start = ((), (), s32[]{:S(2)}) async-start(), calls=%async_computation.3 | async-start | bytes 18874368 | tf_op jit(solution)/shard_map/reduce_scatter | solution.py:50
  1035.5 282.1 %copy-start.3 = (f32[1024]{0:T(1024)S(1)}, f32[1024]{0:T(1024)}, u32[]{:S(2)}) copy-start(f32[1024]{0:T(1024)} %copy-done.2) | copy-start | bytes 12292
Sparse Core Ops, SparseCore 0:
  13.3 637.9 all-gather.1
  1035.6 281.8 reduce-scatter.1
where the time goes:
time: 1330 us
  waiting for transfers between devices  1100 us (83%)
  local copies, waits for them, and re-layouts  128 us (10%)
  matrix products  54.8 us (4%)
  other arithmetic  23.6 us (2%)
  between operations  13.5 us (1%)
    all_gather x1, waiting for transfers between devices, on_device(): whole = lax.all_gather(masked, 'op', axis=0, tiled=True)  637 us
    reduce_scatter x1, waiting for transfers between devices, on_device(): lax.psum_scatter(partial_value, 'op', scatter_dimension=1, tiled=True)  281 us
    all_to_all x1, waiting for transfers between devices, on_device(): lax.all_to_all(blocked, 'bond', split_axis=1, concat_axis=3, tiled=True)  182 us
    dot_general x2, matrix products, on_device(): jnp.einsum('rjpy,jpyz->rjz', chosen, right_blocks[term_idx], preferred_el...  32.1 us
  transfers between devices with their start and end apart: 3, of which 3 were waited for; matrix products, arithmetic and copies ran while one was open for 0% of the time, Pallas kernels for 0%

commit v1 on v0

v1 whole, which is shorter than its diff:
```python
import functools

import jax
import jax.numpy as jnp
from jax import lax
from jax.experimental import pallas as pl
from jax.experimental.pallas import tpu as pltpu
from jax.sharding import PartitionSpec as P

TILE = 128
PAIR = 2
PIECES = 2
VMEM = 48 * 1024 * 1024
MESH = pl.DeviceIdType.MESH
ANY = pl.BlockSpec(memory_space=pl.ANY)


def live_mask(sector_size):
    states = jnp.arange(TILE, dtype=jnp.int32)
    return (states[None, :] < sector_size[:, None]).astype(jnp.float32).reshape(-1)


def gather_kernel(line, wave, left, pairs, whole, lefts, pairs_out, loc_sem, swap_send, swap_recv, line_send, line_recv):
    op = lax.axis_index("op")
    z = op // PAIR
    y = op % PAIR
    partner = z * PAIR + (1 - y)
    rows = wave.shape[0]
    half = wave.shape[1] // PAIR
    cut = rows // PIECES
    barrier = pltpu.get_barrier_semaphore()

    def greet(other):
        pl.semaphore_signal(barrier, inc=1, device_id={"op": other}, device_id_type=MESH)

    greet(partner)

    @pl.when(z > 0)
    def _():
        greet(op - PAIR)

    @pl.when(z < line - 1)
    def _():
        greet(op + PAIR)

    neighbours = 1 + jnp.where(z > 0, 1, 0) + jnp.where(z < line - 1, 1, 0)
    pl.semaphore_wait(barrier, neighbours)

    def remote(src, dst, send, recv, other):
        return pltpu.make_async_remote_copy(
            src_ref=src, dst_ref=dst, send_sem=send, recv_sem=recv, device_id={"op": other}, device_id_type=MESH
        )

    def span(q):
        return pl.ds(q * cut, cut)

    swaps = []
    for q in range(PIECES):
        swaps.append(
            remote(
                wave.at[span(q), pl.ds(pl.multiple_of((1 - y) * half, TILE), half)],
                whole.at[z, y, span(q)],
                swap_send.at[q],
                swap_recv.at[q],
                partner,
            )
        )
    swaps.append(remote(left, lefts.at[y], swap_send.at[PIECES], swap_recv.at[PIECES], partner))
    swaps.append(remote(pairs, pairs_out.at[y], swap_send.at[PIECES + 1], swap_recv.at[PIECES + 1], partner))
    mine = wave.at[:, pl.ds(pl.multiple_of(y * half, TILE), half)]
    locals_ = [
        pltpu.make_async_copy(mine, whole.at[z, y], loc_sem.at[0]),
        pltpu.make_async_copy(left, lefts.at[y], loc_sem.at[1]),
        pltpu.make_async_copy(pairs, pairs_out.at[y], loc_sem.at[2]),
    ]

    def hop(way, step, mate, q):
        source = z - step if way == 0 else z + step
        owner = 1 - y if mate else y
        if step == 0 and not mate:
            src = wave.at[span(q), pl.ds(pl.multiple_of(y * half, TILE), half)]
        else:
            src = whole.at[source, owner, span(q)]
        other = op + PAIR if way == 0 else op - PAIR
        return remote(
            src,
            whole.at[source, owner, span(q)],
            line_send.at[way, step, mate, q],
            line_recv.at[way, step, mate, q],
            other,
        )

    places = (z, line - 1 - z)
    for c in swaps[:PIECES]:
        c.start()
    for step in range(line):
        for mate in range(PAIR):
            for q in range(PIECES):
                if step == 0 and mate:
                    swaps[q].wait_recv()
                for way in range(2):
                    if step > 0:

                        @pl.when(places[way] >= step)
                        def _():
                            hop(way, step - 1, mate, q).wait_recv()

                    if step < line - 1:

                        @pl.when((places[way] >= step) & (places[way] < line - 1))
                        def _():
                            hop(way, step, mate, q).start()

            if step == 0 and not mate:
                for c in swaps[PIECES:] + locals_:
                    c.start()
    for step in range(line - 1):
        for mate in range(PAIR):
            for q in range(PIECES):
                for way in range(2):

                    @pl.when((places[way] >= step) & (places[way] < line - 1))
                    def _():
                        hop(way, step, mate, q).wait_send()

    for c in swaps:
        c.wait_send()
    for c in swaps[PIECES:]:
        c.wait_recv()
    for c in locals_:
        c.wait()


def gather(wave, left, pairs, op_count):
    line = op_count // PAIR
    rows, strip = wave.shape
    hops = (2, max(line - 1, 1), PAIR, PIECES)
    return pl.pallas_call(
        functools.partial(gather_kernel, line),
        out_shape=(
            jax.ShapeDtypeStruct((line, PAIR, rows, strip // PAIR), wave.dtype),
            jax.ShapeDtypeStruct((PAIR,) + left.shape, left.dtype),
            jax.ShapeDtypeStruct((PAIR,) + pairs.shape, pairs.dtype),
        ),
        in_specs=[ANY] * 3,
        out_specs=(ANY,) * 3,
        scratch_shapes=[
            pltpu.SemaphoreType.DMA((3,)),
            pltpu.SemaphoreType.DMA((PIECES + 2,)),
            pltpu.SemaphoreType.DMA((PIECES + 2,)),
            pltpu.SemaphoreType.DMA(hops),
            pltpu.SemaphoreType.DMA(hops),
        ],
        compiler_params=pltpu.CompilerParams(collective_id=0, has_side_effects=True),
        name="gather",
    )(wave, left, pairs)


def exchange_kernel(count, place, target, x, out, loc_sem, send_sem, recv_sem):
    me = place()
    barrier = pltpu.get_barrier_semaphore()
    for d in range(1, count):
        pl.semaphore_signal(barrier, inc=1, device_id=target(lax.rem(me + d, count)), device_id_type=MESH)
    pl.semaphore_wait(barrier, count - 1)
    copies = []
    for d in range(1, count):
        to = lax.rem(me + d, count)
        copies.append(
            pltpu.make_async_remote_copy(
                src_ref=x.at[to],
                dst_ref=out.at[me],
                send_sem=send_sem.at[d],
                recv_sem=recv_sem.at[d],
                device_id=target(to),
                device_id_type=MESH,
            )
        )
    for c in copies:
        c.start()
    own = pltpu.make_async_copy(x.at[me], out.at[me], loc_sem)
    own.start()
    own.wait()
    for c in copies:
        c.wait()


def exchange(x, place, target, cid, name):
    count = x.shape[0]
    return pl.pallas_call(
        functools.partial(exchange_kernel, count, place, target),
        out_shape=jax.ShapeDtypeStruct(x.shape, x.dtype),
        in_specs=[ANY],
        out_specs=ANY,
        scratch_shapes=[
            pltpu.SemaphoreType.DMA,
            pltpu.SemaphoreType.DMA((count,)),
            pltpu.SemaphoreType.DMA((count,)),
        ],
        compiler_params=pltpu.CompilerParams(collective_id=cid, has_side_effects=True),
        name=name,
    )(x)


def plane_place():
    return lax.axis_index("bond") * PAIR + lax.axis_index("op") % PAIR


def plane_target(t):
    return {"bond": t // PAIR, "op": lax.axis_index("op") // PAIR * PAIR + t % PAIR}


def op_place():
    return lax.axis_index("op")


def op_target(t):
    return {"op": t}


def left_kernel(pairs, sizes, blocks, first, second, live, out):
    k, i = pl.program_id(0), pl.program_id(1)
    lane = lax.broadcasted_iota(jnp.int32, (TILE, TILE), 1)
    parts = []
    for p in range(2):
        block = blocks[0, 0, p].astype(jnp.float32)
        parts.append(jnp.where(lane < sizes[pairs[k, i, p]], block, 0.0).astype(jnp.bfloat16))
    a = jnp.concatenate(parts, axis=1)
    b = jnp.concatenate([first[0], second[0]], axis=0)
    out[0, 0] = (jnp.dot(a, b, preferred_element_type=jnp.float32) * live[...]).astype(out.dtype)


def left_product(sectors, lefts, pairs, sizes, live, bond_count):
    mates, terms, outs = lefts.shape[:3]
    half = sectors.shape[2]
    share = outs // bond_count
    blocks = lefts.reshape((mates * terms,) + lefts.shape[2:])
    return pl.pallas_call(
        left_kernel,
        out_shape=jax.ShapeDtypeStruct((bond_count * mates, terms, share * TILE, half), jnp.bfloat16),
        grid_spec=pltpu.PrefetchScalarGridSpec(
            num_scalar_prefetch=2,
            grid=(mates * terms, outs),
            in_specs=[
                pl.BlockSpec((1, 1, 2, TILE, TILE), lambda k, i, pr, sz: (k, i, 0, 0, 0)),
                pl.BlockSpec((1, TILE, half), lambda k, i, pr, sz: (pr[k, i, 0], 0, 0)),
                pl.BlockSpec((1, TILE, half), lambda k, i, pr, sz: (pr[k, i, 1], 0, 0)),
                pl.BlockSpec((1, half), lambda k, i, pr, sz: (0, 0)),
            ],
            out_specs=pl.BlockSpec(
                (1, 1, TILE, half),
                lambda k, i, pr, sz: (i // share * mates + k // terms, k % terms, i % share, 0),
            ),
        ),
        compiler_params=pltpu.CompilerParams(vmem_limit_bytes=VMEM),
        name="left_product",
    )(pairs, sizes, blocks, sectors, sectors, live)


def right_kernel(terms, pairs, blocks, *refs):
    out = refs[-1]
    a = jnp.concatenate([r[0, 0] for r in refs[:-1]], axis=1)
    b = blocks[:, 0].reshape(terms * 2 * TILE, TILE)
    out[0] = jnp.dot(a, b, preferred_element_type=jnp.float32).astype(out.dtype)


def right_product(arrived, right_blocks, pairs, op_count):
    _, terms, share_rows, half = arrived.shape
    sector_count = right_blocks.shape[1]
    per_src = half // TILE
    per_out = sector_count // op_count

    def picked(k, p):
        return pl.BlockSpec(
            (1, 1, share_rows, TILE), lambda j, pr: (pr[k, j, p] // per_src, k, 0, pr[k, j, p] % per_src)
        )

    specs = [picked(k, p) for k in range(terms) for p in range(2)]
    return pl.pallas_call(
        functools.partial(right_kernel, terms),
        out_shape=jax.ShapeDtypeStruct((op_count, share_rows, per_out * TILE), jnp.bfloat16),
        grid_spec=pltpu.PrefetchScalarGridSpec(
            num_scalar_prefetch=1,
            grid=(sector_count,),
            in_specs=[pl.BlockSpec((terms, 1, 2, TILE, TILE), lambda j, pr: (0, j, 0, 0, 0))] + specs,
            out_specs=pl.BlockSpec((1, share_rows, TILE), lambda j, pr: (j // per_out, 0, j % per_out)),
        ),
        compiler_params=pltpu.CompilerParams(vmem_limit_bytes=VMEM),
        name="right_product",
    )(pairs, right_blocks, *([arrived] * len(specs)))


def on_device(wave_slab, left_blocks, right_blocks, sector_size, left_pairs, right_pairs):
    live = live_mask(sector_size)
    op_count = lax.axis_size("op")
    bond_count = lax.axis_size("bond")
    op, bond = lax.axis_index("op"), lax.axis_index("bond")
    strip = wave_slab.shape[1]
    half = strip // PAIR
    flat = left_pairs.reshape(-1)
    padded = -(-flat.size // 1024) * 1024
    sent = jnp.pad(flat, (0, padded - flat.size)).reshape(-1, TILE)
    whole, lefts, both = gather(wave_slab, left_blocks, sent, op_count)
    pairs = both.reshape(PAIR, padded)[:, : flat.size].reshape((-1,) + left_pairs.shape[1:])
    half_live = lax.dynamic_slice_in_dim(live, bond * strip + op % PAIR * half, half)
    middle = left_product(whole.reshape(-1, TILE, half), lefts, pairs, sector_size, half_live[None, :], bond_count)
    arrived = exchange(middle, plane_place, plane_target, 1, "exchange_middle")
    partial = right_product(arrived, right_blocks, right_pairs, op_count)
    got = exchange(partial, op_place, op_target, 2, "exchange_sums")
    summed = jnp.sum(got.astype(jnp.float32), axis=0)
    share_rows, out_cols = summed.shape
    row_live = lax.dynamic_slice_in_dim(live, bond * share_rows, share_rows)
    col_live = lax.dynamic_slice_in_dim(live, op * out_cols, out_cols)
    return summed * row_live[:, None] * col_live[None, :]


def solution(mesh):
    placed = (
        P("op", "bond"),
        P("op", None, None, None, None),
        P("op", None, None, None, None),
        P(),
        P("op", None, None),
        P("op", None, None),
    )
    return jax.shard_map(
        on_device, mesh=mesh, in_specs=placed, out_specs=P("bond", "op"), check_vma=False
    )
```

time: 1330 us -> 756 us (0.57)
  waiting for transfers between devices: 1100 us -> 0 us
  Pallas kernels: 0 us -> 741 us
  local copies, waits for them, and re-layouts: 128 us -> 4.65 us
  matrix products: 54.8 us -> 0 us
  other arithmetic: 23.6 us -> 8.04 us
  between operations: 13.5 us -> 0.08 us
    pallas_call x0 -> x5, Pallas kernels: none -> 741 us  [the longest x2 371 us: exchange(): pl.pallas_call(functools.partial(exchange_kernel, count, place, target),...]
    all_gather x1 -> x0, waiting for transfers between devices: 637 us -> none  [on_device(): whole = lax.all_gather(masked, 'op', axis=0, tiled=True)]
    reduce_scatter x1 -> x0, waiting for transfers between devices: 281 us -> none  [on_device(): lax.psum_scatter(partial_value, 'op', scatter_dimension=1, tiled=True)]
    all_to_all x1 -> x0, waiting for transfers between devices: 182 us -> none  [on_device(): lax.all_to_all(blocked, 'bond', split_axis=1, concat_axis=3, tiled=True)]
    dot_general x4 -> x0, matrix products: 54.8 us -> none  [the longest x2 32.1 us: on_device(): jnp.einsum('rjpy,jpyz->rjz', chosen, right_blocks[term_idx], preferred_el...]
    gather x4 -> x0, local copies, waits for them, and re-layouts: 47.4 us -> none  [the longest x2 24 us: on_device(): picked = sectors[left_pairs[term_idx]]]
    another operation x4 -> x0, local copies, waits for them, and re-layouts: 46.7 us -> none  [the longest x2 23.9 us: on_device(): split_cols = arrived[term_idx, 0].reshape(row_count, sector_count, TILE)]
    reshape x1 -> x3, local copies, waits for them, and re-layouts: 17.4 us -> 0.81 us  [the longest x1 0.6 us: on_device(): sent = jnp.pad(flat, (0, padded - flat.size)).reshape(-1, TILE)]
  transfers between devices with their start and end apart: 3 -> 0, of which waited for: 3 -> 0; matrix products, arithmetic and copies ran while one was open for 0% -> 0% of each run, Pallas kernels for 0% -> 0%
where the time goes in v1:
time: 756 us; the launch traced here: 754 us
  Pallas kernels  741 us (98%)
  other arithmetic  8.04 us (1%)
    pallas_call x2, Pallas kernels, exchange(): pl.pallas_call(functools.partial(exchange_kernel, count, place, target),...  371 us
    pallas_call x1, Pallas kernels, gather(): pl.pallas_call(functools.partial(gather_kernel, line), out_shape=(jax.Sha...  271 us
    pallas_call x1, Pallas kernels, right_product(): pl.pallas_call(functools.partial(right_kernel, terms), out_shape=jax.Shap...  51.5 us
    pallas_call x1, Pallas kernels, left_product(): pl.pallas_call(left_kernel, out_shape=jax.ShapeDtypeStruct((bond_count *...  47.6 us

profile of v1, /device:TPU:13, one launch (start us, length us, event | category | flops | bytes accessed | tf_op | source)
XLA Modules:
  0.0 753.9 jit_solution(1942206261623721887)
XLA Ops:
  0.0 0.0 copy-start.1
  0.0 0.8 convert_bitcast_fusion
  0.8 0.8 copy.9
  1.6 0.1 reshape.27
  1.7 0.6 pad_bitcast_fusion.pairs
  2.3 271.2 %gather.1 = (bf16[4,2,1024,1024]{3,2,1,0:T(8,128)(2,1)}, bf16[2,2,16,2,128,128]{5,4,3,2,1,0:T(8,128)(2,1)}, s32[2,8,128]{2,1,0:T(8,128)}) custom-call(bf16[1024,2048]{1,0:T(8,128)(2,1)} %wave.1, bf16[2,16,2,128,128]{4,3,2,1,0:T(8,128)(2,1)} %left.1, s32[8,128]{1,0:T(8,128)} %pad_bitcast_fusion.pairs), custom_call_target="tpu_custom_call" | custom-call | tf_op jit(solution)/shard_map/gather/pallas_call | solution.py:138
  273.5 0.7 copy.13
  274.2 0.1 reshape.30.pairs
  274.3 0.0 copy-done.1
  274.3 0.0 copy-start
  274.3 2.2 copy-done
  276.5 47.6 %left_product.1.x = bf16[8,2,512,1024]{3,2,1,0:T(8,128)(2,1)} custom-call(s32[4,16,2]{2,1,0:T(8,128)S(1)} %reshape.30.pairs, s32[64]{0:T(128)S(1)} %copy-done.1, bf16[4,16,2,128,128]{4,3,2,1,0:T(8,128)(2,1)S(1)} %bitcast.11, bf16[64,128,1024]{2,1,0:T(8,128)(2,1)} %bitcast.13, bf16[64,128,1024]{2,1,0:T(8,128)(2,1)} %bitcast.14, f32[1,1024]{1,0:T(1,128)S(1)} %bitcast.12), custom_call_target="tpu_custom_call" | custom-call | tf_op jit(solution)/shard_map/left_product/pallas_call | solution.py:237
  324.1 0.0 copy-start.2
  324.1 185.1 %exchange_middle.1.refs_0_.refs_1_.refs_2_.refs_3_ = bf16[8,2,512,1024]{3,2,1,0:T(8,128)(2,1)} custom-call(bf16[8,2,512,1024]{3,2,1,0:T(8,128)(2,1)} %left_product.1.x), custom_call_target="tpu_custom_call" | custom-call | tf_op jit(solution)/shard_map/exchange_middle/pallas_call | solution.py:189
  509.2 0.0 copy-done.2
  509.2 0.1 copy.10.pairs
  509.3 51.5 %right_product.1.x = bf16[8,512,1024]{2,1,0:T(8,128)(2,1)} custom-call(s32[2,64,2]{2,1,0:T(8,128)S(1)} %copy.10.pairs, bf16[2,64,2,128,128]{4,3,2,1,0:T(8,128)(2,1)} %blocks.1, bf16[8,2,512,1024]{3,2,1,0:T(8,128)(2,1)} %exchange_middle.1.refs_0_.refs_1_.refs_2_.refs_3_, bf16[8,2,512,1024]{3,2,1,0:T(8,128)(2,1)} %exchange_middle.1.refs_0_.refs_1_.refs_2_.refs_3_, ...), custom_call_target="tpu_custom_call" | custom-call | tf_op jit(solution)/shard_map/right_product/pallas_call | solution.py:278
  560.8 185.7 %exchange_sums.1 = bf16[8,512,1024]{2,1,0:T(8,128)(2,1)} custom-call(bf16[8,512,1024]{2,1,0:T(8,128)(2,1)} %right_product.1.x), custom_call_target="tpu_custom_call" | custom-call | tf_op jit(solution)/shard_map/exchange_sums/pallas_call | solution.py:189
  746.6 5.7 convert_reduce_fusion
  752.2 0.1 dynamic_slice.10
  752.3 1.6 multiply_multiply_fusion
  (2 shorter events, 0.0 us)
Async XLA Ops:
  0.0 274.3 %copy-start.1 = (s32[64]{0:T(128)S(1)}, s32[64]{0:T(128)}, u32[]{:S(2)}) copy-start(s32[64]{0:T(128)} %sizes.1) | copy-start | bytes 772
  274.3 2.2 copy-start
  324.1 185.1 %copy-start.2 = (s32[2,64,2]{1,2,0:T(2,128)S(1)}, s32[2,64,2]{1,2,0:T(2,128)}, u32[]{:S(2)}) copy-start(s32[2,64,2]{1,2,0:T(2,128)} %param.11) | copy-start | bytes 3076

commit v2 on v1

--- a/solution.py
+++ b/solution.py
@@ -20,7 +20,9 @@
     return (states[None, :] < sector_size[:, None]).astype(jnp.float32).reshape(-1)
 
 
-def gather_kernel(line, wave, left, pairs, whole, lefts, pairs_out, loc_sem, swap_send, swap_recv, line_send, line_recv):
+def gather_kernel(
+    line, wave, left, right, pairs, whole, lefts, rights, pairs_out, loc_sem, swap_send, swap_recv, line_send, line_recv
+):
     op = lax.axis_index("op")
     z = op // PAIR
     y = op % PAIR
@@ -67,11 +69,13 @@
         )
     swaps.append(remote(left, lefts.at[y], swap_send.at[PIECES], swap_recv.at[PIECES], partner))
     swaps.append(remote(pairs, pairs_out.at[y], swap_send.at[PIECES + 1], swap_recv.at[PIECES + 1], partner))
+    swaps.append(remote(right, rights.at[y], swap_send.at[PIECES + 2], swap_recv.at[PIECES + 2], partner))
     mine = wave.at[:, pl.ds(pl.multiple_of(y * half, TILE), half)]
     locals_ = [
         pltpu.make_async_copy(mine, whole.at[z, y], loc_sem.at[0]),
         pltpu.make_async_copy(left, lefts.at[y], loc_sem.at[1]),
         pltpu.make_async_copy(pairs, pairs_out.at[y], loc_sem.at[2]),
+        pltpu.make_async_copy(right, rights.at[y], loc_sem.at[3]),
     ]
 
     def hop(way, step, mate, q):
@@ -131,7 +135,7 @@
         c.wait()
 
 
-def gather(wave, left, pairs, op_count):
+def gather(wave, left, right, pairs, op_count):
     line = op_count // PAIR
     rows, strip = wave.shape
     hops = (2, max(line - 1, 1), PAIR, PIECES)
@@ -140,20 +144,21 @@
         out_shape=(
             jax.ShapeDtypeStruct((line, PAIR, rows, strip // PAIR), wave.dtype),
             jax.ShapeDtypeStruct((PAIR,) + left.shape, left.dtype),
+            jax.ShapeDtypeStruct((PAIR,) + right.shape, right.dtype),
             jax.ShapeDtypeStruct((PAIR,) + pairs.shape, pairs.dtype),
         ),
-        in_specs=[ANY] * 3,
-        out_specs=(ANY,) * 3,
+        in_specs=[ANY] * 4,
+        out_specs=(ANY,) * 4,
         scratch_shapes=[
-            pltpu.SemaphoreType.DMA((3,)),
-            pltpu.SemaphoreType.DMA((PIECES + 2,)),
-            pltpu.SemaphoreType.DMA((PIECES + 2,)),
+            pltpu.SemaphoreType.DMA((4,)),
+            pltpu.SemaphoreType.DMA((PIECES + 3,)),
+            pltpu.SemaphoreType.DMA((PIECES + 3,)),
             pltpu.SemaphoreType.DMA(hops),
             pltpu.SemaphoreType.DMA(hops),
         ],
         compiler_params=pltpu.CompilerParams(collective_id=0, has_side_effects=True),
         name="gather",
-    )(wave, left, pairs)
+    )(wave, left, right, pairs)
 
 
 def exchange_kernel(count, place, target, x, out, loc_sem, send_sem, recv_sem):
@@ -217,76 +222,78 @@
     return {"op": t}
 
 
-def left_kernel(pairs, sizes, blocks, first, second, live, out):
+RESIDENT = dict(pipeline_mode=pl.Buffered(buffer_count=1))
+
+
+def left_kernel(pairs, sizes, blocks, sectors, live, out):
     k, i = pl.program_id(0), pl.program_id(1)
     lane = lax.broadcasted_iota(jnp.int32, (TILE, TILE), 1)
-    parts = []
+    parts, picks = [], []
     for p in range(2):
+        pick = pairs[k, i, p]
         block = blocks[0, 0, p].astype(jnp.float32)
-        parts.append(jnp.where(lane < sizes[pairs[k, i, p]], block, 0.0).astype(jnp.bfloat16))
+        parts.append(jnp.where(lane < sizes[pick], block, 0.0).astype(jnp.bfloat16))
+        picks.append(sectors[pick])
     a = jnp.concatenate(parts, axis=1)
-    b = jnp.concatenate([first[0], second[0]], axis=0)
+    b = jnp.concatenate(picks, axis=0)
     out[0, 0] = (jnp.dot(a, b, preferred_element_type=jnp.float32) * live[...]).astype(out.dtype)
 
 
-def left_product(sectors, lefts, pairs, sizes, live, bond_count):
-    mates, terms, outs = lefts.shape[:3]
+def left_product(sectors, lefts, pairs, sizes, live, plane):
+    terms, outs = lefts.shape[:2]
     half = sectors.shape[2]
-    share = outs // bond_count
-    blocks = lefts.reshape((mates * terms,) + lefts.shape[2:])
+    share = outs // plane
     return pl.pallas_call(
         left_kernel,
-        out_shape=jax.ShapeDtypeStruct((bond_count * mates, terms, share * TILE, half), jnp.bfloat16),
+        out_shape=jax.ShapeDtypeStruct((plane, terms, share * TILE, half), jnp.bfloat16),
         grid_spec=pltpu.PrefetchScalarGridSpec(
             num_scalar_prefetch=2,
-            grid=(mates * terms, outs),
+            grid=(terms, outs),
             in_specs=[
                 pl.BlockSpec((1, 1, 2, TILE, TILE), lambda k, i, pr, sz: (k, i, 0, 0, 0)),
-                pl.BlockSpec((1, TILE, half), lambda k, i, pr, sz: (pr[k, i, 0], 0, 0)),
-                pl.BlockSpec((1, TILE, half), lambda k, i, pr, sz: (pr[k, i, 1], 0, 0)),
+                pl.BlockSpec(sectors.shape, lambda k, i, pr, sz: (0, 0, 0), **RESIDENT),
                 pl.BlockSpec((1, half), lambda k, i, pr, sz: (0, 0)),
             ],
-            out_specs=pl.BlockSpec(
-                (1, 1, TILE, half),
-                lambda k, i, pr, sz: (i // share * mates + k // terms, k % terms, i % share, 0),
-            ),
+            out_specs=pl.BlockSpec((1, 1, TILE, half), lambda k, i, pr, sz: (i // share, k, i % share, 0)),
         ),
         compiler_params=pltpu.CompilerParams(vmem_limit_bytes=VMEM),
         name="left_product",
-    )(pairs, sizes, blocks, sectors, sectors, live)
-
-
-def right_kernel(terms, pairs, blocks, *refs):
-    out = refs[-1]
-    a = jnp.concatenate([r[0, 0] for r in refs[:-1]], axis=1)
+    )(pairs, sizes, lefts, sectors, live)
+
+
+def right_kernel(terms, pairs, blocks, arrived, out):
+    j = pl.program_id(0)
+    per_src = arrived.shape[3] // TILE
+    picks = []
+    for k in range(terms):
+        for p in range(2):
+            s = pairs[k, j, p]
+            lanes = pl.ds(pl.multiple_of(s % per_src * TILE, TILE), TILE)
+            picks.append(arrived[s // per_src, k, :, lanes])
+    a = jnp.concatenate(picks, axis=1)
     b = blocks[:, 0].reshape(terms * 2 * TILE, TILE)
     out[0] = jnp.dot(a, b, preferred_element_type=jnp.float32).astype(out.dtype)
 
 
-def right_product(arrived, right_blocks, pairs, op_count):
-    _, terms, share_rows, half = arrived.shape
-    sector_count = right_blocks.shape[1]
-    per_src = half // TILE
+def right_product(arrived, rights, pairs, op_count):
+    _, terms, rows, _ = arrived.shape
+    sector_count = rights.shape[1]
     per_out = sector_count // op_count
-
-    def picked(k, p):
-        return pl.BlockSpec(
-            (1, 1, share_rows, TILE), lambda j, pr: (pr[k, j, p] // per_src, k, 0, pr[k, j, p] % per_src)
-        )
-
-    specs = [picked(k, p) for k in range(terms) for p in range(2)]
     return pl.pallas_call(
         functools.partial(right_kernel, terms),
-        out_shape=jax.ShapeDtypeStruct((op_count, share_rows, per_out * TILE), jnp.bfloat16),
+        out_shape=jax.ShapeDtypeStruct((op_count, rows, per_out * TILE), jnp.bfloat16),
         grid_spec=pltpu.PrefetchScalarGridSpec(
             num_scalar_prefetch=1,
             grid=(sector_count,),
-            in_specs=[pl.BlockSpec((terms, 1, 2, TILE, TILE), lambda j, pr: (0, j, 0, 0, 0))] + specs,
-            out_specs=pl.BlockSpec((1, share_rows, TILE), lambda j, pr: (j // per_out, 0, j % per_out)),
+            in_specs=[
+                pl.BlockSpec((terms, 1, 2, TILE, TILE), lambda j, pr: (0, j, 0, 0, 0)),
+                pl.BlockSpec(arrived.shape, lambda j, pr: (0, 0, 0, 0), **RESIDENT),
+            ],
+            out_specs=pl.BlockSpec((1, rows, TILE), lambda j, pr: (j // per_out, 0, j % per_out)),
         ),
         compiler_params=pltpu.CompilerParams(vmem_limit_bytes=VMEM),
         name="right_product",
-    )(pairs, right_blocks, *([arrived] * len(specs)))
+    )(pairs, rights, arrived)
 
 
 def on_device(wave_slab, left_blocks, right_blocks, sector_size, left_pairs, right_pairs):
@@ -296,17 +303,23 @@
     op, bond = lax.axis_index("op"), lax.axis_index("bond")
     strip = wave_slab.shape[1]
     half = strip // PAIR
-    flat = left_pairs.reshape(-1)
+    flat = jnp.concatenate([left_pairs.reshape(-1), right_pairs.reshape(-1)])
     padded = -(-flat.size // 1024) * 1024
     sent = jnp.pad(flat, (0, padded - flat.size)).reshape(-1, TILE)
-    whole, lefts, both = gather(wave_slab, left_blocks, sent, op_count)
-    pairs = both.reshape(PAIR, padded)[:, : flat.size].reshape((-1,) + left_pairs.shape[1:])
+    whole, lefts, rights, both = gather(wave_slab, left_blocks, right_blocks, sent, op_count)
+    both = both.reshape(PAIR, padded)
+    lefts_at = both[:, : left_pairs.size].reshape((-1,) + left_pairs.shape[1:])
+    rights_at = both[:, left_pairs.size : flat.size].reshape((-1,) + right_pairs.shape[1:])
+    lefts = lefts.reshape((-1,) + left_blocks.shape[1:])
+    rights = rights.reshape((-1,) + right_blocks.shape[1:])
     half_live = lax.dynamic_slice_in_dim(live, bond * strip + op % PAIR * half, half)
-    middle = left_product(whole.reshape(-1, TILE, half), lefts, pairs, sector_size, half_live[None, :], bond_count)
+    sectors = whole.reshape(-1, TILE, half)
+    middle = left_product(sectors, lefts, lefts_at, sector_size, half_live[None, :], bond_count * PAIR)
     arrived = exchange(middle, plane_place, plane_target, 1, "exchange_middle")
-    partial = right_product(arrived, right_blocks, right_pairs, op_count)
+    partial = right_product(arrived, rights, rights_at, op_count)
     got = exchange(partial, op_place, op_target, 2, "exchange_sums")
-    summed = jnp.sum(got.astype(jnp.float32), axis=0)
+    got = got.reshape((-1, PAIR) + got.shape[1:])
+    summed = jnp.sum(got.astype(jnp.float32), axis=0).reshape(-1, got.shape[3])
     share_rows, out_cols = summed.shape
     row_live = lax.dynamic_slice_in_dim(live, bond * share_rows, share_rows)
     col_live = lax.dynamic_slice_in_dim(live, op * out_cols, out_cols)

time: 756 us -> 765 us (1.012)
  Pallas kernels: 741 us -> 751 us
    pallas_call x1, Pallas kernels: 271 us -> 384 us  [gather(): pl.pallas_call(functools.partial(gather_kernel, line), out_shape=(jax.Sha...]
    pallas_call x2, Pallas kernels: 371 us -> 279 us  [exchange(): pl.pallas_call(functools.partial(exchange_kernel, count, place, target),...]
    pallas_call x1, Pallas kernels: 47.6 us -> 37.5 us  [left_product(): pl.pallas_call(left_kernel, out_shape=jax.ShapeDtypeStruct((plane, terms,...]
where the time goes in v2:
time: 765 us; the launch traced here: 764 us
  Pallas kernels  751 us (98%)
    pallas_call x1, Pallas kernels, gather(): pl.pallas_call(functools.partial(gather_kernel, line), out_shape=(jax.Sha...  384 us
    pallas_call x2, Pallas kernels, exchange(): pl.pallas_call(functools.partial(exchange_kernel, count, place, target),...  279 us
    pallas_call x1, Pallas kernels, right_product(): pl.pallas_call(functools.partial(right_kernel, terms), out_shape=jax.Shap...  50.4 us
    pallas_call x1, Pallas kernels, left_product(): pl.pallas_call(left_kernel, out_shape=jax.ShapeDtypeStruct((plane, terms,...  37.5 us

profile of v2, /device:TPU:13, one launch (start us, length us, event | category | flops | bytes accessed | tf_op | source)
XLA Modules:
  0.0 764.3 jit_solution(10476539965651555535)
XLA Ops:
  0.0 0.8 copy.8
  0.8 0.1 reshape.42
  0.9 0.7 convert_bitcast_fusion
  1.6 0.1 dynamic_slice.10
  1.7 0.8 copy.9
  2.5 0.1 reshape.43
  2.6 0.1 pad_add_fusion
  2.7 0.6 pad_bitcast_fusion.pairs
  3.3 0.0 copy-start.2
  3.3 384.2 %gather.1 = (bf16[4,2,1024,1024]{3,2,1,0:T(8,128)(2,1)}, bf16[2,2,16,2,128,128]{5,4,3,2,1,0:T(8,128)(2,1)}, bf16[2,2,64,2,128,128]{5,4,3,2,1,0:T(8,128)(2,1)}, s32[2,8,128]{2,1,0:T(8,128)}) custom-call(bf16[1024,2048]{1,0:T(8,128)(2,1)} %wave.1, bf16[2,16,2,128,128]{4,3,2,1,0:T(8,128)(2,1)} %left.1, bf16[2,64,2,128,128]{4,3,2,1,0:T(8,128)(2,1)} %right.1, ...), custom_call_target="tpu_custom_call" | custom-call | tf_op jit(solution)/shard_map/gather/pallas_call | solution.py:142
  387.5 0.7 copy.12
  388.3 0.1 slice.8
  388.3 0.1 reshape.48.pairs
  388.4 0.0 copy-done.2
  388.4 0.0 copy-start.1
  388.5 2.2 copy-done.1
  390.6 37.5 %left_product.1.x = bf16[8,4,256,1024]{3,2,1,0:T(8,128)(2,1)} custom-call(s32[4,16,2]{2,1,0:T(8,128)S(1)} %reshape.48.pairs, s32[64]{0:T(128)S(1)} %copy-done.2, bf16[4,16,2,128,128]{4,3,2,1,0:T(8,128)(2,1)S(1)} %bitcast.18, bf16[64,128,1024]{2,1,0:T(8,128)(2,1)} %bitcast.21, f32[1,1024]{1,0:T(1,128)S(1)} %bitcast.19), custom_call_target="tpu_custom_call" | custom-call | tf_op jit(solution)/shard_map/left_product/pallas_call | solution.py:246
  428.1 184.5 %exchange_middle.1.arrived = bf16[8,4,256,1024]{3,2,1,0:T(8,128)(2,1)} custom-call(bf16[8,4,256,1024]{3,2,1,0:T(8,128)(2,1)} %left_product.1.x), custom_call_target="tpu_custom_call" | custom-call | tf_op jit(solution)/shard_map/exchange_middle/pallas_call | solution.py:194
  612.6 0.1 reshape.46.pairs
  612.8 50.4 %right_product.1.x = bf16[8,256,1024]{2,1,0:T(8,128)(2,1)S(1)} custom-call(s32[4,64,2]{2,1,0:T(8,128)S(1)} %reshape.46.pairs, bf16[4,64,2,128,128]{4,3,2,1,0:T(8,128)(2,1)} %bitcast.20, bf16[8,4,256,1024]{3,2,1,0:T(8,128)(2,1)} %exchange_middle.1.arrived), custom_call_target="tpu_custom_call" | custom-call | tf_op jit(solution)/shard_map/right_product/pallas_call | solution.py:282
  663.1 0.0 copy-start
  663.1 1.9 copy-done
  665.1 94.3 %exchange_sums.1 = bf16[8,256,1024]{2,1,0:T(8,128)(2,1)} custom-call(bf16[8,256,1024]{2,1,0:T(8,128)(2,1)} %copy-done), custom_call_target="tpu_custom_call" | custom-call | tf_op jit(solution)/shard_map/exchange_sums/pallas_call | solution.py:194
  759.4 3.4 convert_reduce_fusion
  762.8 1.6 fusion
  (2 shorter events, 0.0 us)
Async XLA Ops:
  3.3 385.1 %copy-start.2 = (s32[64]{0:T(128)S(1)}, s32[64]{0:T(128)}, u32[]{:S(2)}) copy-start(s32[64]{0:T(128)} %sizes.1) | copy-start | bytes 772
  388.4 2.2 copy-start.1
  663.1 1.9 copy-start

commit v3 on v2

--- a/solution.py
+++ b/solution.py
@@ -10,6 +10,7 @@
 TILE = 128
 PAIR = 2
 PIECES = 2
+SLICES = 8
 VMEM = 48 * 1024 * 1024
 MESH = pl.DeviceIdType.MESH
 ANY = pl.BlockSpec(memory_space=pl.ANY)
@@ -69,7 +70,13 @@
         )
     swaps.append(remote(left, lefts.at[y], swap_send.at[PIECES], swap_recv.at[PIECES], partner))
     swaps.append(remote(pairs, pairs_out.at[y], swap_send.at[PIECES + 1], swap_recv.at[PIECES + 1], partner))
-    swaps.append(remote(right, rights.at[y], swap_send.at[PIECES + 2], swap_recv.at[PIECES + 2], partner))
+    part = right.shape[1] // SLICES
+    for n in range(SLICES):
+        some = pl.ds(n * part, part)
+        place = PIECES + 2 + n
+        swaps.append(
+            remote(right.at[:, some], rights.at[y, :, some], swap_send.at[place], swap_recv.at[place], partner)
+        )
     mine = wave.at[:, pl.ds(pl.multiple_of(y * half, TILE), half)]
     locals_ = [
         pltpu.make_async_copy(mine, whole.at[z, y], loc_sem.at[0]),
@@ -97,6 +104,7 @@
     places = (z, line - 1 - z)
     for c in swaps[:PIECES]:
         c.start()
+    waiting = swaps[PIECES + 2 :] + swaps[PIECES : PIECES + 2] + locals_
     for step in range(line):
         for mate in range(PAIR):
             for q in range(PIECES):
@@ -115,9 +123,11 @@
                         def _():
                             hop(way, step, mate, q).start()
 
-            if step == 0 and not mate:
-                for c in swaps[PIECES:] + locals_:
-                    c.start()
+                if waiting:
+                    waiting.pop(0).start()
+
+    for c in waiting:
+        c.start()
     for step in range(line - 1):
         for mate in range(PAIR):
             for q in range(PIECES):
@@ -151,8 +161,8 @@
         out_specs=(ANY,) * 4,
         scratch_shapes=[
             pltpu.SemaphoreType.DMA((4,)),
-            pltpu.SemaphoreType.DMA((PIECES + 3,)),
-            pltpu.SemaphoreType.DMA((PIECES + 3,)),
+            pltpu.SemaphoreType.DMA((PIECES + 2 + SLICES,)),
+            pltpu.SemaphoreType.DMA((PIECES + 2 + SLICES,)),
             pltpu.SemaphoreType.DMA(hops),
             pltpu.SemaphoreType.DMA(hops),
         ],

time: 765 us -> 926 us (1.21)
  Pallas kernels: 751 us -> 911 us
    pallas_call x1, Pallas kernels: 384 us -> 543 us  [gather(): pl.pallas_call(functools.partial(gather_kernel, line), out_shape=(jax.Sha...]
where the time goes in v3:
time: 926 us; the launch traced here: 925 us
  Pallas kernels  911 us (98%)
    pallas_call x1, Pallas kernels, gather(): pl.pallas_call(functools.partial(gather_kernel, line), out_shape=(jax.Sha...  543 us
    pallas_call x2, Pallas kernels, exchange(): pl.pallas_call(functools.partial(exchange_kernel, count, place, target),...  280 us
    pallas_call x1, Pallas kernels, right_product(): pl.pallas_call(functools.partial(right_kernel, terms), out_shape=jax.Shap...  50.4 us
    pallas_call x1, Pallas kernels, left_product(): pl.pallas_call(left_kernel, out_shape=jax.ShapeDtypeStruct((plane, terms,...  37.5 us

profile of v3, /device:TPU:13, one launch (start us, length us, event | category | flops | bytes accessed | tf_op | source)
XLA Modules:
  0.0 924.7 jit_solution(11209280696828869367)
XLA Ops:
  0.0 0.8 copy.8
  0.8 0.1 reshape.42
  0.9 0.7 convert_bitcast_fusion
  1.6 0.1 dynamic_slice.10
  1.7 0.8 copy.9
  2.5 0.1 reshape.43
  2.6 0.1 pad_add_fusion
  2.7 0.6 pad_bitcast_fusion.pairs
  3.3 0.0 copy-start.2
  3.3 543.4 %gather.1 = (bf16[4,2,1024,1024]{3,2,1,0:T(8,128)(2,1)}, bf16[2,2,16,2,128,128]{5,4,3,2,1,0:T(8,128)(2,1)}, bf16[2,2,64,2,128,128]{5,4,3,2,1,0:T(8,128)(2,1)}, s32[2,8,128]{2,1,0:T(8,128)}) custom-call(bf16[1024,2048]{1,0:T(8,128)(2,1)} %wave.1, bf16[2,16,2,128,128]{4,3,2,1,0:T(8,128)(2,1)} %left.1, bf16[2,64,2,128,128]{4,3,2,1,0:T(8,128)(2,1)} %right.1, ...), custom_call_target="tpu_custom_call" | custom-call | tf_op jit(solution)/shard_map/gather/pallas_call | solution.py:152
  546.7 0.7 copy.12
  547.4 0.1 slice.8
  547.5 0.1 reshape.48.pairs
  547.6 0.0 copy-done.2
  547.6 0.0 copy-start.1
  547.6 2.2 copy-done.1
  549.8 37.5 %left_product.1.x = bf16[8,4,256,1024]{3,2,1,0:T(8,128)(2,1)} custom-call(s32[4,16,2]{2,1,0:T(8,128)S(1)} %reshape.48.pairs, s32[64]{0:T(128)S(1)} %copy-done.2, bf16[4,16,2,128,128]{4,3,2,1,0:T(8,128)(2,1)S(1)} %bitcast.18, bf16[64,128,1024]{2,1,0:T(8,128)(2,1)} %bitcast.21, f32[1,1024]{1,0:T(1,128)S(1)} %bitcast.19), custom_call_target="tpu_custom_call" | custom-call | tf_op jit(solution)/shard_map/left_product/pallas_call | solution.py:256
  587.3 186.2 %exchange_middle.1.arrived = bf16[8,4,256,1024]{3,2,1,0:T(8,128)(2,1)} custom-call(bf16[8,4,256,1024]{3,2,1,0:T(8,128)(2,1)} %left_product.1.x), custom_call_target="tpu_custom_call" | custom-call | tf_op jit(solution)/shard_map/exchange_middle/pallas_call | solution.py:204
  773.5 0.1 reshape.46.pairs
  773.7 50.4 %right_product.1.x = bf16[8,256,1024]{2,1,0:T(8,128)(2,1)S(1)} custom-call(s32[4,64,2]{2,1,0:T(8,128)S(1)} %reshape.46.pairs, bf16[4,64,2,128,128]{4,3,2,1,0:T(8,128)(2,1)} %bitcast.20, bf16[8,4,256,1024]{3,2,1,0:T(8,128)(2,1)} %exchange_middle.1.arrived), custom_call_target="tpu_custom_call" | custom-call | tf_op jit(solution)/shard_map/right_product/pallas_call | solution.py:292
  824.0 0.0 copy-start
  824.1 1.9 copy-done
  826.0 93.8 %exchange_sums.1 = bf16[8,256,1024]{2,1,0:T(8,128)(2,1)} custom-call(bf16[8,256,1024]{2,1,0:T(8,128)(2,1)} %copy-done), custom_call_target="tpu_custom_call" | custom-call | tf_op jit(solution)/shard_map/exchange_sums/pallas_call | solution.py:204
  919.8 3.4 convert_reduce_fusion
  923.2 1.6 fusion
  (2 shorter events, 0.0 us)
Async XLA Ops:
  3.3 544.3 %copy-start.2 = (s32[64]{0:T(128)S(1)}, s32[64]{0:T(128)}, u32[]{:S(2)}) copy-start(s32[64]{0:T(128)} %sizes.1) | copy-start | bytes 772
  547.6 2.2 copy-start.1
  824.0 1.9 copy-start
